TPU v7x, 32 devices: a whole 2x2x4 slice. The times are simulated.
32 devices in a mesh: across: 4 (over y, x), along: 8 (over z, core).
Axes of the slice: x: 2, y: 2, z: 4, core: 2. Of those that a mesh axis runs over, the one named last changes fastest.
Arguments:
- radiance: bfloat16 [224, 128, 2048], P(None, 'along', 'across'), as said below
- kernel_one: float32 [224, 25], replicated, may hold values from 0 to 0.08
- kernel_two: float32 [224, 25], replicated, may hold values from 0 to 0.08
- usable_mask: int32 [128, 2048], P('along', 'across'), may hold values from 0 to 1, as said below
Outputs:
- anomaly_score: float32 [128, 2048], P('along', 'across')
Inputs may be any that keep to these rules, and one draw needn't show every extreme that they name: `usable_mask`: 1 marks a pixel that enters the statistics and is scored, 0 one that is left out. Calibrated radiance, finite.
All inputs are finite; a program needn't handle non-finite values.
Results may differ from a plain program's by a relative error of at most 0.0019.
Values may be sent and summed in bfloat16 or wider, within the bound.
A program may use at most 128 MiB of HBM per device.

v0:
```python
import math

import jax
import jax.numpy as jnp
from jax import lax
from jax.sharding import PartitionSpec as P

KSIZE = 5


def padded_2(block, sides, width):
    for axis, dim in sides:
        count = lax.axis_size(axis)
        forward = [(i, i + 1) for i in range(count - 1)]
        backward = [(target, source) for source, target in forward]
        low = lax.ppermute(
            lax.slice_in_dim(block, block.shape[dim] - width, None, axis=dim), axis, forward
        )
        high = lax.ppermute(lax.slice_in_dim(block, 0, width, axis=dim), axis, backward)
        block = jnp.concatenate([low, block, high], axis=dim)
    return block


def smooth(padded, kernel, out_rows, out_cols):
    total = jnp.zeros((padded.shape[0], out_rows, out_cols), jnp.float32)
    for tap in range(KSIZE * KSIZE):
        row_off, col_off = divmod(tap, KSIZE)
        window = padded[:, row_off : row_off + out_rows, col_off : col_off + out_cols]
        total = total + kernel[:, tap][:, None, None] * window
    return total


def per_device(radiance, kernel_one, kernel_two, usable_mask):
    band_count, tile_rows, tile_cols = radiance.shape
    reach = KSIZE // 2
    widened = padded_2(radiance, (("across", 2), ("along", 1)), reach)
    section_one = smooth(widened.astype(jnp.float32), kernel_one, tile_rows, tile_cols)
    section_wide = padded_2(section_one, (("across", 2), ("along", 1)), reach)
    section_two = smooth(section_wide, kernel_two, tile_rows, tile_cols)
    smoothed = section_two.astype(jnp.bfloat16)
    masked = smoothed * usable_mask.astype(jnp.bfloat16)[None]
    flat = masked.reshape(band_count, tile_rows * tile_cols)
    local_count = jnp.sum(usable_mask.astype(jnp.float32))
    local_sum = jnp.sum(flat, axis=1, dtype=jnp.float32)
    local_gram = lax.dot_general(
        flat, flat, (((1,), (1,)), ((), ())), preferred_element_type=jnp.float32
    )
    count, band_sum, gram = lax.psum((local_count, local_sum, local_gram), ("across", "along"))
    global_mean = band_sum / count
    covariance = (gram - count * jnp.outer(global_mean, global_mean)) / (count - 1.0)
    loading = 0.01 * jnp.trace(covariance) / band_count
    loaded = covariance + loading * jnp.eye(band_count, dtype=jnp.float32)
    lower = jnp.linalg.cholesky(loaded)
    whitener = lax.linalg.triangular_solve(
        lower, jnp.eye(band_count, dtype=jnp.float32), left_side=True, lower=True
    )
    centered = (
        smoothed.astype(jnp.float32).reshape(band_count, tile_rows * tile_cols)
        - global_mean[:, None]
    )
    whitened = jnp.dot(
        whitener, centered, precision=lax.Precision.HIGHEST, preferred_element_type=jnp.float32
    )
    distance = jnp.sum(whitened * whitened, axis=0).reshape(tile_rows, tile_cols)
    standard = (distance - band_count) / math.sqrt(2.0 * band_count)
    return standard * usable_mask.astype(jnp.float32)


def solution(mesh):
    in_specs = (P(None, "along", "across"), P(), P(), P("along", "across"))
    out_specs = P("along", "across")
    return jax.shard_map(
        per_device, mesh=mesh, in_specs=in_specs, out_specs=out_specs, check_vma=False
    )
```

profile of v0, /device:TPU:0, one launch (start us, length us, event | category | flops | bytes accessed | tf_op | source)
XLA Modules:
  0.0 480.5 jit_solution(15867702169217414534)
XLA Ops:
  6.5 1.9 fusion.78
  8.4 0.8 copy.24
  9.2 4.8 %collective-permute-start = (bf16[224,16,2]{0,1,2:T(8,128)(2,1)S(1)}, bf16[224,16,2]{0,1,2:T(8,128)(2,1)S(1)}, u32[]{:S(2)}, u32[]{:S(2)}) collective-permute-start(bf16[224,16,2]{0,1,2:T(8,128)(2,1)S(1)} %copy.24), channel_id=1, source_target_pairs={{0,8},{8,16},{16,24},{1,9},{9,17},{17,25},{2,10},{10,18},{18,26},{... | collective-permute-start | bytes 43016 | tf_op jit(solution)/shard_map/ppermute | solution.py:16
  14.1 0.8 copy.25
  14.9 1.3 collective-permute-start.1
  16.2 7.4 %copy.11 = bf16[224,16,512]{0,2,1:T(8,128)(2,1)} copy(bf16[224,16,512]{2,1,0:T(8,128)(2,1)} %param.4) | data formatting | bytes 7340032 | tf_op args[0]
  23.6 1.5 pad_maximum_fusion.8
  25.1 1.5 collective-permute-start.2
  26.6 1.3 collective-permute-start.3
  28.0 0.1 collective-permute-done.2
  28.1 3.9 collective-permute-done.3
  32.0 7.9 %maximum_convert_fusion = f32[224,20,516]{0,2,1:T(8,128)} fusion(bf16[224,2,516]{0,2,1:T(8,128)(2,1)S(1)} %collective-permute-done.3, bf16[224,16,2]{0,2,1:T(2,128)(2,1)S(1)} %copy.12, bf16[224,16,512]{0,2,1:T(8,128)(2,1)} %copy.11, bf16[224,16,2]{0,2,1:T(2,128)(2,1)S(1)} %copy.10, bf16[224,2,516]{0,2,1:T(8,128)(2,1)S(1)} %collective-permute-done.2), kind=kLoop, calls=%fused_computation.111 | loop fusion | flops 23116800 | bytes 13870080 | tf_op jit(solution)/shard_map/convert_element_type | solution.py:37
  39.9 80.4 %fusion.30 = f32[224,16,512]{0,2,1:T(8,128)} fusion(f32[224,20,516]{0,2,1:T(8,128)} %maximum_convert_fusion, f32[224]{0:T(256)S(1)} %bitcast.109, f32[224]{0:T(256)S(1)} %bitcast.110, f32[224]{0:T(256)S(1)} %bitcast.112, f32[224]{0:T(256)S(1)} %bitcast.113, f32[224]{0:T(256)S(1)} %bitcast.114, f32[224]{0:T(256)S(1)} %bitcast.115, f32[224]{0:T(256)S(1)} %bitcast.116, ...), kind=kLoop, calls=%fused_computation.60 | loop fusion | flops 89915392 | bytes 190863232 | tf_op jit(solution)/shard_map/add | solution.py:29
  120.3 1.1 fusion.77
  121.5 4.8 %collective-permute-start.4 = (f32[224,16,2]{0,1,2:T(8,128)S(1)}, f32[224,16,2]{0,1,2:T(8,128)S(1)}, u32[]{:S(2)}, u32[]{:S(2)}) collective-permute-start(f32[224,16,2]{0,1,2:T(8,128)S(1)} %copy.13), channel_id=1, source_target_pairs={{0,8},{8,16},{16,24},{1,9},{9,17},{17,25},{2,10},{10,18},{18,26},{... | collective-permute-start | bytes 86024 | tf_op jit(solution)/shard_map/ppermute | solution.py:16
  126.3 1.3 collective-permute-start.5
  127.6 0.3 collective-permute-done.4
  127.9 4.6 collective-permute-done.5
  132.5 1.7 pad_maximum_fusion.5
  134.3 8.1 %collective-permute-start.6 = (f32[224,2,516]{0,2,1:T(8,128)S(1)}, f32[224,2,516]{0,2,1:T(8,128)S(1)}, u32[]{:S(2)}, u32[]{:S(2)}) collective-permute-start(f32[224,2,516]{0,2,1:T(8,128)S(1)} %get-tuple-element.31), channel_id=1, source_target_pairs={{0,1},{1,2},{2,3},{3,4},{4,5},{5,6},{6,7},{8,9},{9,10},{10,11},{11... | collective-permute-start | bytes 2774024 | tf_op jit(solution)/shard_map/ppermute | solution.py:16
  142.4 1.5 collective-permute-start.7
  143.9 0.6 convert_reduce_fusion.1
  144.6 2.8 collective-permute-done.7
  147.4 8.7 %maximum_maximum_fusion = (f32[224,18,516]{0,2,1:T(8,128)}, f32[224,18,516]{0,2,1:T(8,128)}) fusion(f32[224,16,2]{0,2,1:T(2,128)S(1)} %copy.16, f32[224,16,512]{0,2,1:T(8,128)S(1)} %copy-done, f32[224,16,2]{0,2,1:T(2,128)S(1)} %copy.15, f32[224,2,516]{0,2,1:T(8,128)S(1)} %collective-permute-done.6, f32[224,2,516]{0,2,1:T(8,128)S(1)} %collective-permute-done.7), kind=kLoop, calls=%fused_computation.1 | loop fusion | flops 12483072 | bytes 25890816 | tf_op jit(solution)/shard_map/concatenate | solution.py:20
  156.1 98.0 %convert_reduce_fusion = (f32[224]{0:T(256)S(1)}, bf16[224,16,512]{0,2,1:T(8,128)(2,1)}) fusion(bf16[16,512]{1,0:T(8,128)(2,1)S(1)} %convert_element_type.22, f32[224,18,516]{0,2,1:T(8,128)} %get-tuple-element.30, f32[224]{0:T(256)S(1)} %bitcast.84, f32[224]{0:T(256)S(1)} %bitcast.85, f32[224]{0:T(256)S(1)} %bitcast.87, f32[224]{0:T(256)S(1)} %bitcast.88, ...), kind=kLoop, calls=%fused_computation.109 | loop fusion | flops 104595232 | bytes 157907712 | tf_op jit(solution)/shard_map/reduce_sum | solution.py:44
  254.1 7.1 %fusion.60 = f32[224,224]{1,0:T(8,128)} fusion(bf16[224,16,512]{0,2,1:T(8,128)(2,1)} %get-tuple-element.28, bf16[16,512]{1,0:T(8,128)(2,1)S(1)} %convert_element_type.22), kind=kOutput, calls=%fused_computation.117 | convolution fusion | flops 823918592 | bytes 3887104 | tf_op jit(solution)/shard_map/dot_general | solution.py:45
  261.2 0.0 all-reduce.6.cloned.1.call-update
  261.2 53.2 %all-reduce.3 = (f32[224]{0:T(256)S(1)}, f32[]{:T(128)}) all-reduce(f32[224]{0:T(256)S(1)} %get-tuple-element.27, f32[]{:T(128)} %convert_reduce_fusion.1), channel_id=1, replica_groups=mesh['across'=4,'along'=8] {'across','along'}, use_global_device_ids=true, to_apply=%region_4.0 | all-reduce | flops 225 | bytes 1800 | tf_op jit(solution)/shard_map/psum | solution.py:48
  314.4 0.6 broadcast_divide_fusion
  315.7 81.4 %all-reduce.6.cloned.1.call-done = f32[224,224]{1,0:T(8,128)} async-done(((f32[224,224]{1,0:T(8,128)}), f32[224,224]{1,0:T(8,128)}) %all-reduce.6.cloned.1.call-update) | async-done | bytes 200720 | tf_op jit(solution)/shard_map/psum | solution.py:48
  397.0 2.3 select_reduce_fusion
  400.0 1.7 select_add_fusion
  401.7 0.1 copy.21
  401.8 1.7 fusion.66
  403.5 11.7 %cholesky.50 = f32[128,128]{1,0:T(8,128)S(1)} custom-call(f32[128,128]{1,0:T(8,128)S(1)} %cholesky.121), custom_call_target="Cholesky" | custom-call | tf_op jit(solution)/shard_map/jit(cholesky)/cholesky | solution.py:53
  415.3 9.8 %custom-call.14 = f32[1,128,128]{1,2,0:T(8,128)S(1)} custom-call(f32[1,128,128]{2,1,0:T(8,128)S(1)} %get-tuple-element.40), custom_call_target="InvertDiagBlocksLowerTriangular" | custom-call | tf_op jit(solution)/shard_map/jit(cholesky)/cholesky | solution.py:53
  425.1 0.2 constant_dynamic-update-slice_fusion.1
  425.3 0.2 convolution_subtract_fusion.1
  425.6 8.8 %cholesky.108 = f32[96,96]{1,0:T(8,128)S(1)} custom-call(f32[96,96]{1,0:T(8,128)S(1)} %convolution_subtract_fusion.1), custom_call_target="Cholesky" | custom-call | tf_op jit(solution)/shard_map/jit(cholesky)/cholesky | solution.py:53
  434.4 0.6 compare_reduce_fusion
  435.0 0.6 compare_reduce_fusion.1
  436.9 0.1 fusion.69
  437.0 19.9 %custom-call.15 = f32[2,128,128]{1,2,0:T(8,128)S(1)} custom-call(f32[2,128,128]{2,1,0:T(8,128)S(1)} %pad_maximum_fusion.9), custom_call_target="InvertDiagBlocksLowerTriangular" | custom-call | tf_op jit(solution)/shard_map/triangular_solve | solution.py:54
  457.0 0.3 fusion.67
  457.3 0.4 convolution_subtract_fusion
  457.6 0.4 fusion.73
  458.0 15.0 %fusion.59 = f32[8192]{0:T(1024)S(1)} fusion(bf16[224,8192]{0,1:T(8,128)(2,1)} %bitcast.79, f32[224]{0:T(256)S(1)} %broadcast_divide_fusion, f32[96,224]{0,1:T(8,128)S(1)} %fusion.73, f32[128,224]{0,1:T(8,128)S(1)} %fusion.67), kind=kOutput, calls=%fused_computation.116 | convolution fusion | flops 4939883520 | bytes 3904384 | tf_op jit(solution)/shard_map/dot_general | solution.py:61
  473.0 0.6 convert_multiply_fusion
  (35 shorter events, 0.4 us)
Async XLA Ops:
  6.5 390.5 %all-reduce.6.cloned.1.call-start = ((), (), s32[]{:S(2)}) async-start(), calls=%async_computation | async-start | bytes 458752 | tf_op jit(solution)/shard_map/psum | solution.py:48
  8.4 19.5 %copy-start.2 = (f32[224,25]{0,1:T(8,128)S(1)}, f32[224,25]{0,1:T(8,128)}, u32[]{:S(2)}) copy-start(f32[224,25]{0,1:T(8,128)} %param.5) | copy-start | bytes 67204
  9.2 14.3 %collective-permute-start = (bf16[224,16,2]{0,1,2:T(8,128)(2,1)S(1)}, bf16[224,16,2]{0,1,2:T(8,128)(2,1)S(1)}, u32[]{:S(2)}, u32[]{:S(2)}) collective-permute-start(bf16[224,16,2]{0,1,2:T(8,128)(2,1)S(1)} %copy.24), channel_id=1, source_target_pairs={{0,8},{8,16},{16,24},{1,9},{9,17},{17,25},{2,10},{10,18},{18,26},{... | collective-permute-start | bytes 43016 | tf_op jit(solution)/shard_map/ppermute | solution.py:16
  14.9 8.7 %collective-permute-start.1 = (bf16[224,16,2]{0,1,2:T(8,128)(2,1)S(1)}, bf16[224,16,2]{0,1,2:T(8,128)(2,1)S(1)}, u32[]{:S(2)}, u32[]{:S(2)}) collective-permute-start(bf16[224,16,2]{0,1,2:T(8,128)(2,1)S(1)} %copy.25), channel_id=1, source_target_pairs={{8,0},{16,8},{24,16},{9,1},{17,9},{25,17},{10,2},{18,10},{26,18},{... | collective-permute-start | bytes 43016 | tf_op jit(solution)/shard_map/ppermute | solution.py:19
  25.1 3.0 collective-permute-start.2
  26.6 5.4 %collective-permute-start.3 = (bf16[224,2,516]{0,2,1:T(8,128)(2,1)S(1)}, bf16[224,2,516]{0,2,1:T(8,128)(2,1)S(1)}, u32[]{:S(2)}, u32[]{:S(2)}) collective-permute-start(bf16[224,2,516]{0,2,1:T(8,128)(2,1)S(1)} %get-tuple-element.36), channel_id=1, source_target_pairs={{1,0},{2,1},{3,2},{4,3},{5,4},{6,5},{7,6},{9,8},{10,9},{11,10},{12... | collective-permute-start | bytes 1387016 | tf_op jit(solution)/shard_map/ppermute | solution.py:19
  120.3 23.6 %copy-start.1 = (s32[16,512]{1,0:T(8,128)S(1)}, s32[16,512]{1,0:T(8,128)}, u32[]{:S(2)}) copy-start(s32[16,512]{1,0:T(8,128)} %param.7) | copy-start | bytes 98308
  120.3 24.3 %copy-start.3 = (f32[224,25]{0,1:T(8,128)S(1)}, f32[224,25]{0,1:T(8,128)}, u32[]{:S(2)}) copy-start(f32[224,25]{0,1:T(8,128)} %param.6) | copy-start | bytes 67204
  120.3 27.1 %copy-start = (f32[224,16,512]{0,2,1:T(8,128)S(1)}, f32[224,16,512]{0,2,1:T(8,128)}, u32[]{:S(2)}) copy-start(f32[224,16,512]{0,2,1:T(8,128)} %fusion.30) | copy-start | bytes 22020100
  121.5 6.4 %collective-permute-start.4 = (f32[224,16,2]{0,1,2:T(8,128)S(1)}, f32[224,16,2]{0,1,2:T(8,128)S(1)}, u32[]{:S(2)}, u32[]{:S(2)}) collective-permute-start(f32[224,16,2]{0,1,2:T(8,128)S(1)} %copy.13), channel_id=1, source_target_pairs={{0,8},{8,16},{16,24},{1,9},{9,17},{17,25},{2,10},{10,18},{18,26},{... | collective-permute-start | bytes 86024 | tf_op jit(solution)/shard_map/ppermute | solution.py:16
  126.3 6.2 %collective-permute-start.5 = (f32[224,16,2]{0,1,2:T(8,128)S(1)}, f32[224,16,2]{0,1,2:T(8,128)S(1)}, u32[]{:S(2)}, u32[]{:S(2)}) collective-permute-start(f32[224,16,2]{0,1,2:T(8,128)S(1)} %copy.14), channel_id=1, source_target_pairs={{8,0},{16,8},{24,16},{9,1},{17,9},{25,17},{10,2},{18,10},{26,18},{... | collective-permute-start | bytes 86024 | tf_op jit(solution)/shard_map/ppermute | solution.py:19
  134.3 10.3 %collective-permute-start.6 = (f32[224,2,516]{0,2,1:T(8,128)S(1)}, f32[224,2,516]{0,2,1:T(8,128)S(1)}, u32[]{:S(2)}, u32[]{:S(2)}) collective-permute-start(f32[224,2,516]{0,2,1:T(8,128)S(1)} %get-tuple-element.31), channel_id=1, source_target_pairs={{0,1},{1,2},{2,3},{3,4},{4,5},{5,6},{6,7},{8,9},{9,10},{10,11},{11... | collective-permute-start | bytes 2774024 | tf_op jit(solution)/shard_map/ppermute | solution.py:16
  142.4 5.0 %collective-permute-start.7 = (f32[224,2,516]{0,2,1:T(8,128)S(1)}, f32[224,2,516]{0,2,1:T(8,128)S(1)}, u32[]{:S(2)}, u32[]{:S(2)}) collective-permute-start(f32[224,2,516]{0,2,1:T(8,128)S(1)} %get-tuple-element.32), channel_id=1, source_target_pairs={{1,0},{2,1},{3,2},{4,3},{5,4},{6,5},{7,6},{9,8},{10,9},{11,10},{12... | collective-permute-start | bytes 2774024 | tf_op jit(solution)/shard_map/ppermute | solution.py:19
Sparse Core Ops, SparseCore 0:
  261.3 135.6 all-reduce.5
where the time goes:
time: 482 us; the launch traced here: 480 us
  other arithmetic  257 us (53%)
  waiting for transfers between devices  93.1 us (19%)
  blocking collectives  53.2 us (11%)
  starting transfers between devices  24.6 us (5%)
  matrix products  23.6 us (5%)
  between operations  16.3 us (3%)
  local copies, waits for them, and re-layouts  12.3 us (3%)
    reduce_sum x1, other arithmetic, per_device(): local_sum = jnp.sum(flat, axis=1, dtype=jnp.float32)  98 us
    psum x1, waiting for transfers between devices, per_device(): lax.psum((local_count, local_sum, local_gram), ('across', 'along'))  81.4 us
    add x1, other arithmetic, smooth(): total = total + kernel[:, tap][:, None, None] * window  80.4 us
    psum x1, blocking collectives, per_device(): lax.psum((local_count, local_sum, local_gram), ('across', 'along'))  53.2 us
    another operation x7, other arithmetic, per_device(): lower = jnp.linalg.cholesky(loaded)  31.6 us
    another operation x6, other arithmetic, per_device(): lax.linalg.triangular_solve(lower, jnp.eye(band_count, dtype=jnp.float32)...  20.1 us
    ppermute x4, starting transfers between devices, padded_2(): lax.ppermute(lax.slice_in_dim(block, block.shape[dim] - width, None, axis...  19.2 us
    dot_general x1, matrix products, per_device(): jnp.dot(whitener, centered, precision=lax.Precision.HIGHEST, preferred_el...  15 us
  transfers between devices with their start and end apart: 9, of which 6 were waited for; matrix products, arithmetic and copies ran while one was open for 2% of the time, Pallas kernels for 0%

commit v1 on v0

v1 whole, which is shorter than its diff:
```python
import functools
import math

import jax
import jax.numpy as jnp
import numpy as np
from jax import lax
from jax.experimental import pallas as pl
from jax.experimental.pallas import tpu as pltpu
from jax.sharding import PartitionSpec as P

KSIZE = 5
REACH = KSIZE // 2
HALO = 2 * REACH
GROUP = 16
SIDE = 256
MESH_ID = pl.DeviceIdType.MESH


def row_orders(rows):
    packed_in = list(range(rows)) + list(range(-HALO, 0)) + list(range(rows, rows + HALO))
    packed_mid = list(range(rows)) + list(range(-REACH, 0)) + list(range(rows, rows + REACH))
    packed_mid += [None] * (-len(packed_mid) % 8)
    return packed_in, packed_mid


def tap_selector(out_order, in_order):
    select = np.zeros((KSIZE, KSIZE * len(out_order), len(in_order)), np.float32)
    for q in range(KSIZE):
        for m, r in enumerate(out_order):
            for k, s in enumerate(in_order):
                if r is not None and s is not None and 0 <= s - r + REACH < KSIZE:
                    select[s - r + REACH, q * len(out_order) + m, k] = 1.0
    return select


def tap_matrix(kernel, out_order, in_order, parts, width):
    bands = kernel.shape[0]
    high = lax.reduce_precision(kernel, 8, 7)
    low = kernel - high
    one = tap_selector(out_order, in_order)
    select = np.zeros((KSIZE, one.shape[1], width), np.float32)
    is_low = np.zeros((1, 1, width), bool)
    n = len(in_order)
    for i, part in enumerate(parts):
        select[:, :, i * n : (i + 1) * n] = one
        is_low[:, :, i * n : (i + 1) * n] = part == "low"

    def spread(taps, p):
        row = taps[:, p * KSIZE : (p + 1) * KSIZE]
        return jnp.repeat(row, len(out_order), axis=1)[:, :, None]

    total = jnp.zeros((bands, one.shape[1], width), jnp.float32)
    for p in range(KSIZE):
        total = total + select[p][None] * jnp.where(is_low, spread(low, p), spread(high, p))
    return total.astype(jnp.bfloat16)


def smooth_kernel(main_ref, halo_ref, edge_ref, first_ref, second_ref, keep_ref, out_ref, hold):
    rows, cols = main_ref.shape[1:]
    wide = cols + edge_ref.shape[2]
    mid = keep_ref.shape[0]

    def gather_columns(product, count):
        total = product[REACH * count : (REACH + 1) * count, :]
        for q in range(KSIZE):
            if q != REACH:
                total = total + pltpu.roll(
                    product[q * count : (q + 1) * count, :], (REACH - q) % wide, 1
                )
        return total

    def one_band(b, carry):
        main = jnp.concatenate([main_ref[b], edge_ref[b]], axis=1).astype(jnp.float32)
        packed = jnp.concatenate([main, halo_ref[b].astype(jnp.float32)], axis=0)
        packed = jnp.concatenate([packed, packed], axis=0).astype(jnp.bfloat16)
        product = jnp.dot(first_ref[b], packed, preferred_element_type=jnp.float32)
        section = gather_columns(product, mid) * keep_ref[...]
        high = section.astype(jnp.bfloat16).astype(jnp.float32)
        low = section - high
        spare = second_ref.shape[2] - 3 * mid
        packed = jnp.concatenate(
            [high, low, high, jnp.zeros((spare, wide), jnp.float32)], axis=0
        ).astype(jnp.bfloat16)
        product = jnp.dot(second_ref[b], packed, preferred_element_type=jnp.float32)
        result = gather_columns(product, rows)
        for j in range(cols // 128):
            hold[j, pl.ds(pl.multiple_of(b * rows, rows), rows), :] = result[:, j * 128 : j * 128 + 128]
        return carry

    lax.fori_loop(0, GROUP, one_band, 0, unroll=4)
    for r in range(rows):
        for j in range(cols // 128):
            out_ref[r, :, j * 128 : j * 128 + 128] = hold[
                j, pl.ds(r, GROUP, stride=rows), :
            ].astype(jnp.bfloat16)


def smooth_twice(radiance, halo, edge, first, second, keep):
    bands, rows, cols = radiance.shape

    def band_block(array):
        return pl.BlockSpec((GROUP,) + array.shape[1:], lambda i: (i, 0, 0))

    return pl.pallas_call(
        smooth_kernel,
        grid=(bands // GROUP,),
        out_shape=jax.ShapeDtypeStruct((rows, bands, cols), jnp.bfloat16),
        in_specs=[band_block(a) for a in (radiance, halo, edge, first, second)]
        + [pl.BlockSpec(keep.shape, lambda i: (0, 0))],
        out_specs=pl.BlockSpec((rows, GROUP, cols), lambda i: (0, i, 0)),
        scratch_shapes=[pltpu.VMEM((cols // 128, GROUP * rows, 128), jnp.float32)],
        compiler_params=pltpu.CompilerParams(vmem_limit_bytes=40 << 20),
        name="smooth_twice",
    )(radiance, halo, edge, first, second, keep)


def gram_kernel(x_ref, mask_ref, out_ref):
    step = pl.program_id(0)
    bands, cols = x_ref.shape[1:]
    per = x_ref.shape[0]

    @pl.when(step == 0)
    def _():
        out_ref[...] = jnp.zeros_like(out_ref)

    first = lax.broadcasted_iota(jnp.int32, (SIDE - bands, cols), 0) == 0
    total = jnp.zeros((SIDE, SIDE), jnp.float32)
    for r in range(per):
        line = mask_ref[r : r + 1, :].astype(jnp.float32)
        used = jnp.broadcast_to(line, (bands, cols)).astype(jnp.bfloat16)
        ones = jnp.where(first, jnp.broadcast_to(line, first.shape), 0.0).astype(jnp.bfloat16)
        block = jnp.concatenate([x_ref[r] * used, ones], axis=0)
        total = total + lax.dot_general(
            block, block, (((1,), (1,)), ((), ())), preferred_element_type=jnp.float32
        )
    out_ref[...] += total


def local_gram(smoothed, mask):
    rows, bands, cols = smoothed.shape
    per = 8
    return pl.pallas_call(
        gram_kernel,
        grid=(rows // per,),
        out_shape=jax.ShapeDtypeStruct((SIDE, SIDE), jnp.float32),
        in_specs=[
            pl.BlockSpec((per, bands, cols), lambda i: (i, 0, 0)),
            pl.BlockSpec((per, cols), lambda i: (i, 0)),
        ],
        out_specs=pl.BlockSpec((SIDE, SIDE), lambda i: (0, 0)),
        compiler_params=pltpu.CompilerParams(vmem_limit_bytes=40 << 20),
        name="local_gram",
    )(smoothed, mask)


def sum_kernel(
    na, nl, x_ref, out_ref, near, part, far, full, s1, r1, s2, r2, s3, r3, s4, r4
):
    ma, ml = lax.axis_index("across"), lax.axis_index("along")
    barrier = pltpu.get_barrier_semaphore()
    for axis, me, n in (("across", ma, na), ("along", ml, nl)):
        for d in range(1, n):
            pl.semaphore_signal(
                barrier, inc=1, device_id={axis: lax.rem(me + d, n)}, device_id_type=MESH_ID
            )
    pl.semaphore_wait(barrier, na - 1 + nl - 1)

    big = SIDE // na
    owners = min(nl, big // 8)
    small = big // owners

    def rows_of(start, count):
        return pl.ds(pl.multiple_of(start, 8), count)

    def copy(src, dst, send, recv, axis, peer):
        return pltpu.make_async_remote_copy(
            src_ref=src, dst_ref=dst, send_sem=send, recv_sem=recv,
            device_id={axis: peer}, device_id_type=MESH_ID,
        )

    def owner_only(index, action):
        if owners == nl:
            action()
        else:
            pl.when(index < owners)(action)

    one = []
    for d in range(1, na):
        peer = lax.rem(ma + d, na)
        one.append(copy(x_ref.at[rows_of(peer * big, big)], near.at[d - 1],
                        s1.at[d - 1], r1.at[d - 1], "across", peer))
    for c in one:
        c.start()
    for c in one:
        c.wait_recv()
    total = x_ref[rows_of(ma * big, big), :]
    for d in range(1, na):
        total = total + near[d - 1]
    part[...] = total

    two = []
    for d in range(1, nl):
        peer = lax.rem(ml + d, nl)
        slot = peer if owners == nl else lax.rem(peer, owners)
        two.append((peer, copy(part.at[rows_of(slot * small, small)], far.at[d - 1],
                               s2.at[d - 1], r2.at[d - 1], "along", peer)))
    for peer, c in two:
        owner_only(peer, c.start)

    mine = ml if owners == nl else lax.rem(ml, owners)
    here = rows_of(ma * big + mine * small, small)

    three = []
    for d in range(1, nl):
        peer = lax.rem(ml + d, nl)
        three.append(copy(full.at[here], full.at[here], s3.at[d - 1], r3.at[d - 1], "along", peer))

    def reduce_mine():
        for _, c in two:
            c.wait_recv()
        total = part[rows_of(mine * small, small), :]
        for d in range(1, nl):
            total = total + far[d - 1]
        full[here, :] = total
        for c in three:
            c.start()

    owner_only(ml, reduce_mine)
    for d in range(1, nl):
        owner_only(lax.rem(ml - d + nl, nl), three[d - 1].wait_recv)

    four = []
    block = rows_of(ma * big, big)
    for d in range(1, na):
        peer = lax.rem(ma + d, na)
        four.append(copy(full.at[block], full.at[block], s4.at[d - 1], r4.at[d - 1], "across", peer))
    for c in four:
        c.start()
    for c in four:
        c.wait_recv()
    out_ref[...] = full[...]
    for c in one:
        c.wait_send()
    for peer, c in two:
        owner_only(peer, c.wait_send)

    def sent():
        for c in three:
            c.wait_send()

    owner_only(ml, sent)
    for c in four:
        c.wait_send()


def sum_everywhere(gram):
    na, nl = lax.axis_size("across"), lax.axis_size("along")
    big = SIDE // na
    owners = min(nl, big // 8)
    dma = pltpu.SemaphoreType.DMA
    return pl.pallas_call(
        functools.partial(sum_kernel, na, nl),
        out_shape=jax.ShapeDtypeStruct(gram.shape, jnp.float32),
        in_specs=[pl.BlockSpec(memory_space=pltpu.VMEM)],
        out_specs=pl.BlockSpec(memory_space=pltpu.VMEM),
        scratch_shapes=[
            pltpu.VMEM((na - 1, big, SIDE), jnp.float32),
            pltpu.VMEM((big, SIDE), jnp.float32),
            pltpu.VMEM((nl - 1, big // owners, SIDE), jnp.float32),
            pltpu.VMEM((SIDE, SIDE), jnp.float32),
            dma((na - 1,)), dma((na - 1,)),
            dma((nl - 1,)), dma((nl - 1,)),
            dma((nl - 1,)), dma((nl - 1,)),
            dma((na - 1,)), dma((na - 1,)),
        ],
        compiler_params=pltpu.CompilerParams(collective_id=1, has_side_effects=True),
        name="sum_everywhere",
    )(gram)


def score_kernel(high_ref, low_ref, shift_ref, x_ref, mask_ref, out_ref):
    bands = high_ref.shape[0]
    for r in range(x_ref.shape[0]):
        x = x_ref[r]
        white = jnp.dot(high_ref[...], x, preferred_element_type=jnp.float32)
        white = white + jnp.dot(low_ref[...], x, preferred_element_type=jnp.float32)
        white = white - shift_ref[...]
        distance = jnp.sum(white * white, axis=0, keepdims=True)
        standard = (distance - bands) * (1.0 / math.sqrt(2.0 * bands))
        out_ref[r : r + 1, :] = standard * mask_ref[r : r + 1, :].astype(jnp.float32)


def score(whitener, mean, smoothed, mask):
    rows, bands, cols = smoothed.shape
    per = 8
    high = lax.reduce_precision(whitener, 8, 7)
    low = (whitener - high).astype(jnp.bfloat16)
    shift = jnp.dot(whitener, mean[:, None], precision=lax.Precision.HIGHEST)
    square = pl.BlockSpec((bands, bands), lambda i: (0, 0))
    lines = pl.BlockSpec((per, cols), lambda i: (i, 0))
    return pl.pallas_call(
        score_kernel,
        grid=(rows // per,),
        out_shape=jax.ShapeDtypeStruct((rows, cols), jnp.float32),
        in_specs=[
            square, square, pl.BlockSpec((bands, 1), lambda i: (0, 0)),
            pl.BlockSpec((per, bands, cols), lambda i: (i, 0, 0)), lines,
        ],
        out_specs=lines,
        compiler_params=pltpu.CompilerParams(vmem_limit_bytes=40 << 20),
        name="score",
    )(high.astype(jnp.bfloat16), low, shift, smoothed, mask)


def from_sides(low_edge, high_edge, axis):
    count = lax.axis_size(axis)
    forward = [(i, i + 1) for i in range(count - 1)]
    backward = [(i + 1, i) for i in range(count - 1)]
    return lax.ppermute(high_edge, axis, forward), lax.ppermute(low_edge, axis, backward)


def per_device(radiance, kernel_one, kernel_two, usable_mask):
    bands, rows, cols = radiance.shape
    na, nl = lax.axis_size("across"), lax.axis_size("along")
    ma, ml = lax.axis_index("across"), lax.axis_index("along")
    left, right = from_sides(radiance[:, :, :HALO], radiance[:, :, cols - HALO :], "across")
    above, below = from_sides(radiance[:, :HALO, :], radiance[:, rows - HALO :, :], "along")
    corner = jnp.concatenate([right, left], axis=2)
    corner_above, corner_below = from_sides(corner[:, :HALO], corner[:, rows - HALO :], "along")

    def widen(sides):
        gap = jnp.zeros(sides.shape[:2] + (128 - 2 * HALO,), sides.dtype)
        return jnp.concatenate([sides[:, :, :HALO], gap, sides[:, :, HALO:]], axis=2)

    edge = widen(corner)
    halo = jnp.concatenate(
        [jnp.concatenate([above, below], axis=1),
         widen(jnp.concatenate([corner_above, corner_below], axis=1))], axis=2)

    in_order, mid_order = row_orders(rows)
    first = tap_matrix(kernel_one, mid_order, in_order, ("high", "low"), 2 * len(in_order))
    packed = 3 * len(mid_order)
    second = tap_matrix(kernel_two, list(range(rows)), mid_order, ("high", "high", "low"),
                        packed + (-packed % 16))
    row_at = jnp.asarray([0 if r is None else r for r in mid_order], jnp.int32)[:, None]
    col_at = jnp.arange(cols + 128, dtype=jnp.int32)[None, :]
    col_at = jnp.where(col_at < cols + 64, col_at, col_at - cols - 128)
    row_at, col_at = row_at + ml * rows, col_at + ma * cols
    keep = (row_at >= 0) & (row_at < nl * rows) & (col_at >= 0) & (col_at < na * cols)
    smoothed = smooth_twice(radiance, halo, edge, first, second, keep.astype(jnp.float32))

    whole = sum_everywhere(local_gram(smoothed, usable_mask))
    gram, band_sum, count = whole[:bands, :bands], whole[bands, :bands], whole[bands, bands]
    mean = band_sum / count
    covariance = (gram - count * jnp.outer(mean, mean)) / (count - 1.0)
    loading = 0.01 * jnp.trace(covariance) / bands
    loaded = covariance + loading * jnp.eye(bands, dtype=jnp.float32)
    lower = jnp.linalg.cholesky(loaded)
    whitener = lax.linalg.triangular_solve(
        lower, jnp.eye(bands, dtype=jnp.float32), left_side=True, lower=True
    )
    return score(whitener, mean, smoothed, usable_mask)


def solution(mesh):
    in_specs = (P(None, "along", "across"), P(), P(), P("along", "across"))
    out_specs = P("along", "across")
    return jax.shard_map(
        per_device, mesh=mesh, in_specs=in_specs, out_specs=out_specs, check_vma=False
    )
```

time: 482 us -> 280 us (0.58)
  other arithmetic: 257 us -> 128 us
  Pallas kernels: 0 us -> 112 us
  waiting for transfers between devices: 93.1 us -> 0.83 us
  blocking collectives: 53.2 us -> 0 us
  matrix products: 23.6 us -> 1.66 us
  between operations: 16.3 us -> 3.53 us
  starting transfers between devices: 24.6 us -> 16 us
  local copies, waits for them, and re-layouts: 12.3 us -> 18.2 us
    pallas_call x0 -> x4, Pallas kernels: none -> 112 us  [the longest x1 82.1 us: smooth_twice(): pl.pallas_call(smooth_kernel, grid=(bands // GROUP,), out_shape=jax.Shape...]
    reduce_sum x3 -> x1, other arithmetic: 101 us -> 2.3 us  [per_device(): loading = 0.01 * jnp.trace(covariance) / bands]
    psum x1 -> x0, waiting for transfers between devices: 81.4 us -> none  [per_device(): lax.psum((local_count, local_sum, local_gram), ('across', 'along'))]
    add x2 -> x1, other arithmetic: 82 us -> 1.69 us  [per_device(): loaded = covariance + loading * jnp.eye(bands, dtype=jnp.float32)]
    convert_element_type x2 -> x4, other arithmetic: 7.9 us -> 65.4 us  [the longest x2 65.3 us: tap_matrix(): return total.astype(jnp.bfloat16)]
    psum x1 -> x0, blocking collectives: 53.2 us -> none  [per_device(): lax.psum((local_count, local_sum, local_gram), ('across', 'along'))]
    dot_general x2 -> x1, matrix products: 22.1 us -> 0.32 us  [score(): shift = jnp.dot(whitener, mean[:, None], precision=lax.Precision.HIGHEST)]
    ppermute x8 -> x6, waiting for transfers between devices: 11.7 us -> 0.83 us  [the longest x3 0.82 us: from_sides(): lax.ppermute(low_edge, axis, backward)]
  transfers between devices with their start and end apart: 9 -> 6, of which waited for: 6 -> 1; matrix products, arithmetic and copies ran while one was open for 2% -> 27% of each run, Pallas kernels for 0% -> 0%
where the time goes in v1:
time: 280 us
  other arithmetic  128 us (46%)
  Pallas kernels  112 us (40%)
  local copies, waits for them, and re-layouts  18.2 us (6%)
  starting transfers between devices  16 us (6%)
  between operations  3.53 us (1%)
    pallas_call x1, Pallas kernels, smooth_twice(): pl.pallas_call(smooth_kernel, grid=(bands // GROUP,), out_shape=jax.Shape...  82.1 us
    convert_element_type x2, other arithmetic, tap_matrix(): return total.astype(jnp.bfloat16)  65.3 us
    another operation x7, other arithmetic, per_device(): lower = jnp.linalg.cholesky(loaded)  31.7 us
    pallas_call x1, Pallas kernels, sum_everywhere(): pl.pallas_call(functools.partial(sum_kernel, na, nl), out_shape=jax.Shape...  25.3 us
    another operation x6, other arithmetic, per_device(): lax.linalg.triangular_solve(lower, jnp.eye(bands, dtype=jnp.float32), lef...  20 us
    ppermute x3, starting transfers between devices, from_sides(): lax.ppermute(high_edge, axis, forward)  12.1 us
    unnamed x43, local copies, waits for them, and re-layouts  6.26 us
  transfers between devices with their start and end apart: 6, of which 1 were waited for; matrix products, arithmetic and copies ran while one was open for 27% of the time, Pallas kernels for 0%

profile of v1, /device:TPU:0, one launch (start us, length us, event | category | flops | bytes accessed | tf_op | source)
XLA Modules:
  0.0 279.7 jit_solution(12012104639165992291)
XLA Ops:
  0.0 1.9 fusion.16
  2.0 0.8 copy.94
  2.8 1.3 collective-permute-start.2
  4.1 0.8 copy.95
  4.9 5.5 %collective-permute-start.3 = (bf16[224,16,4]{0,1,2:T(8,128)(2,1)S(1)}, bf16[224,16,4]{0,1,2:T(8,128)(2,1)S(1)}, u32[]{:S(2)}, u32[]{:S(2)}) collective-permute-start(bf16[224,16,4]{0,1,2:T(8,128)(2,1)S(1)} %copy.95), channel_id=1, source_target_pairs={{0,8},{8,16},{16,24},{1,9},{9,17},{17,25},{2,10},{10,18},{18,26},{... | collective-permute-start | bytes 86024 | tf_op jit(solution)/shard_map/ppermute | solution.py:320
  10.4 4.1 %fusion.15 = (bf16[224,4,512]{2,1,0:T(4,128)(2,1)}, bf16[224,4,512]{2,1,0:T(4,128)(2,1)}) fusion(bf16[224,16,512]{2,1,0:T(8,128)(2,1)} %main_ref.1), kind=kLoop, calls=%fused_computation.60 | loop fusion | bytes 3670016 | tf_op jit(solution)/shard_map/slice | solution.py:328
  14.5 2.4 collective-permute-start
  16.9 1.3 collective-permute-start.1
  19.6 0.1 copy.81
  19.7 0.1 copy.82
  19.8 0.1 copy.83
  20.8 39.0 %add_convert_fusion.first_ref = bf16[224,120,48]{2,1,0:T(8,128)(2,1)} fusion(f32[224,120]{1,0:T(8,128)S(1)} %copy.80, f32[224,120]{1,0:T(8,128)S(1)} %copy.79, f32[120,48]{1,0:T(8,128)S(1)} %copy-done.9, f32[224,120]{1,0:T(8,128)S(1)} %copy.78, f32[224,120]{1,0:T(8,128)S(1)} %copy.77, f32[120,48]{1,0:T(8,128)S(1)} %copy-done.8, f32[224,120]{1,0:T(8,128)S(1)} %copy.76, ...), kind=kLoop, calls=%fused_computation | loop fusion | flops 19353600 | bytes 3770928 | tf_op jit(solution)/shard_map/convert_element_type | solution.py:56
  59.9 26.3 %add_convert_fusion.1.second_ref = bf16[224,80,80]{2,1,0:T(8,128)(2,1)} fusion(f32[224,80]{1,0:T(8,128)S(1)} %copy.90, f32[224,80]{1,0:T(8,128)S(1)} %copy.89, f32[80,80]{1,0:T(8,128)S(1)} %copy-done.14, f32[224,80]{1,0:T(8,128)S(1)} %copy.88, f32[224,80]{1,0:T(8,128)S(1)} %copy.87, f32[80,80]{1,0:T(8,128)S(1)} %copy-done.13, f32[224,80]{1,0:T(8,128)S(1)} %copy.86, ...), kind=kLoop, calls=%fused_computation.1 | loop fusion | flops 21504000 | bytes 3712080 | tf_op jit(solution)/shard_map/convert_element_type | solution.py:56
  86.5 4.3 %collective-permute-start.4 = (bf16[224,4,8]{0,2,1:T(8,128)(2,1)S(1)}, bf16[224,4,8]{0,2,1:T(8,128)(2,1)S(1)}, u32[]{:S(2)}, u32[]{:S(2)}) collective-permute-start(bf16[224,4,8]{0,2,1:T(8,128)(2,1)S(1)} %get-tuple-element.34), channel_id=1, source_target_pairs={{0,1},{1,2},{2,3},{3,4},{4,5},{5,6},{6,7},{8,9},{9,10},{10,11},{11... | collective-permute-start | bytes 43016 | tf_op jit(solution)/shard_map/ppermute | solution.py:320
  90.8 1.3 collective-permute-start.5
  92.1 0.8 copy.69
  92.9 0.8 copy.70
  93.7 0.6 pad_maximum_fusion.1.edge_ref
  94.3 0.8 collective-permute-done.5
  95.1 0.3 copy.67
  95.4 0.3 copy.68
  95.8 2.9 %pad_maximum_fusion.halo_ref = bf16[224,8,640]{2,1,0:T(8,128)(2,1)S(1)} fusion(bf16[224,8,4]{2,1,0:T(8,128)(2,1)S(1)} %copy.68, bf16[224,8,4]{2,1,0:T(8,128)(2,1)S(1)} %copy.67, bf16[224,4,512]{2,1,0:T(4,128)(2,1)} %collective-permute-done.1, bf16[224,4,512]{2,1,0:T(4,128)(2,1)} %collective-permute-done, bf16[640]{0:T(1024)(128)(2,1)S(1)} %pad.20.clone), kind=kLoop, calls=%fused_computation.2 | loop fusion | flops 11468800 | bytes 4158720 | tf_op jit(solution)/shard_map/concatenate | solution.py:337
  98.7 82.1 %smooth_twice.1.x_ref = bf16[16,224,512]{2,1,0:T(8,128)(2,1)S(1)} custom-call(bf16[224,16,512]{2,1,0:T(8,128)(2,1)S(1)} %copy-done.2, bf16[224,8,640]{2,1,0:T(8,128)(2,1)S(1)} %pad_maximum_fusion.halo_ref, bf16[224,16,128]{2,1,0:T(8,128)(2,1)S(1)} %pad_maximum_fusion.1.edge_ref, bf16[224,120,48]{2,1,0:T(8,128)(2,1)} %add_convert_fusion.first_ref, ...), custom_call_target="tpu_custom_call" | custom-call | tf_op jit(solution)/shard_map/smooth_twice/pallas_call | solution.py:105
  180.8 1.5 local_gram.1.x_ref
  182.4 1.8 copy-done
  184.1 0.7 copy-done.3
  184.8 25.3 %sum_everywhere.1 = f32[256,256]{1,0:T(8,128)} custom-call(f32[256,256]{1,0:T(8,128)} %copy-done.3), custom_call_target="tpu_custom_call" | custom-call | tf_op jit(solution)/shard_map/sum_everywhere/pallas_call | solution.py:262
  210.1 1.3 slice.167
  211.4 1.3 slice_divide_fusion
  213.4 2.3 select_reduce_fusion
  216.3 1.7 select_add_fusion
  218.0 0.1 copy.91
  218.1 1.7 fusion.1
  219.9 11.7 %cholesky.50 = f32[128,128]{1,0:T(8,128)S(1)} custom-call(f32[128,128]{1,0:T(8,128)S(1)} %cholesky.121), custom_call_target="Cholesky" | custom-call | tf_op jit(solution)/shard_map/jit(cholesky)/cholesky | solution.py:359
  231.6 9.8 %custom-call.14 = f32[1,128,128]{1,2,0:T(8,128)S(1)} custom-call(f32[1,128,128]{2,1,0:T(8,128)S(1)} %get-tuple-element.32), custom_call_target="InvertDiagBlocksLowerTriangular" | custom-call | tf_op jit(solution)/shard_map/jit(cholesky)/cholesky | solution.py:359
  241.5 0.2 constant_dynamic-update-slice_fusion.3
  241.7 0.2 convolution_subtract_fusion.1
  241.9 8.8 %cholesky.108 = f32[96,96]{1,0:T(8,128)S(1)} custom-call(f32[96,96]{1,0:T(8,128)S(1)} %convolution_subtract_fusion.1), custom_call_target="Cholesky" | custom-call | tf_op jit(solution)/shard_map/jit(cholesky)/cholesky | solution.py:359
  250.7 0.7 compare_reduce_fusion
  251.4 0.6 compare_reduce_fusion.1
  253.5 19.9 %custom-call.15 = f32[2,128,128]{1,2,0:T(8,128)S(1)} custom-call(f32[2,128,128]{2,1,0:T(8,128)S(1)} %pad_maximum_fusion.4), custom_call_target="InvertDiagBlocksLowerTriangular" | custom-call | tf_op jit(solution)/shard_map/triangular_solve | solution.py:360
  273.4 0.3 fusion.2
  273.7 0.4 convolution_subtract_fusion
  274.0 0.1 copy.92
  274.1 0.3 fusion.8
  274.4 0.3 convolution_bitcast_fusion.shift_ref
  274.8 2.0 copy-done.1
  276.8 2.9 %score.1 = f32[16,512]{1,0:T(8,128)} custom-call(bf16[224,224]{1,0:T(8,128)(2,1)S(1)} %get-tuple-element.30.high_ref, bf16[224,224]{1,0:T(8,128)(2,1)S(1)} %get-tuple-element.29.low_ref, f32[224,1]{1,0:T(8,128)S(1)} %convolution_bitcast_fusion.shift_ref, bf16[16,224,512]{2,1,0:T(8,128)(2,1)S(1)} %copy-done.1, s32[16,512]{1,0:T(8,128)S(1)} %copy-done.4), custom_call_target="tpu_custom_call" | custom-call | tf_op jit(solution)/shard_map/score/pallas_call | solution.py:302
  (108 shorter events, 2.5 us)
Async XLA Ops:
  0.0 18.2 %copy-start.15 = (f32[224,25]{0,1:T(8,128)S(1)}, f32[224,25]{0,1:T(8,128)}, u32[]{:S(2)}) copy-start(f32[224,25]{0,1:T(8,128)} %param.18) | copy-start | bytes 67204
  0.0 19.5 %copy-start.16 = (f32[224,25]{0,1:T(8,128)S(1)}, f32[224,25]{0,1:T(8,128)}, u32[]{:S(2)}) copy-start(f32[224,25]{0,1:T(8,128)} %param.19) | copy-start | bytes 67204
  1.9 18.8 %copy-start.19 = (s32[24]{0:T(128)S(1)}, s32[24]{0:T(128)}, u32[]{:S(2)}) copy-start(s32[24]{0:T(128)} %constant.162.clone) | copy-start | bytes 292
  1.9 18.9 %copy-start.5 = (f32[120,48]{1,0:T(8,128)S(1)}, f32[120,48]{1,0:T(8,128)}, u32[]{:S(2)}) copy-start(f32[120,48]{1,0:T(8,128)} %constant.194) | copy-start | bytes 69124
  1.9 18.9 %copy-start.6 = (f32[120,48]{1,0:T(8,128)S(1)}, f32[120,48]{1,0:T(8,128)}, u32[]{:S(2)}) copy-start(f32[120,48]{1,0:T(8,128)} %constant.196) | copy-start | bytes 69124
  1.9 18.9 %copy-start.7 = (f32[120,48]{1,0:T(8,128)S(1)}, f32[120,48]{1,0:T(8,128)}, u32[]{:S(2)}) copy-start(f32[120,48]{1,0:T(8,128)} %constant.197) | copy-start | bytes 69124
  2.0 18.9 %copy-start.8 = (f32[120,48]{1,0:T(8,128)S(1)}, f32[120,48]{1,0:T(8,128)}, u32[]{:S(2)}) copy-start(f32[120,48]{1,0:T(8,128)} %constant.198) | copy-start | bytes 69124
  2.0 18.9 %copy-start.9 = (f32[120,48]{1,0:T(8,128)S(1)}, f32[120,48]{1,0:T(8,128)}, u32[]{:S(2)}) copy-start(f32[120,48]{1,0:T(8,128)} %constant.199) | copy-start | bytes 69124
  2.0 18.9 %copy-start.18 = (pred[48]{0:T(512)(128)(4,1)S(1)}, pred[48]{0:T(512)(128)(4,1)}, u32[]{:S(2)}) copy-start(pred[48]{0:T(512)(128)(4,1)} %constant.195) | copy-start | bytes 148
  2.8 83.6 %collective-permute-start.2 = (bf16[224,16,4]{0,1,2:T(8,128)(2,1)S(1)}, bf16[224,16,4]{0,1,2:T(8,128)(2,1)S(1)}, u32[]{:S(2)}, u32[]{:S(2)}) collective-permute-start(bf16[224,16,4]{0,1,2:T(8,128)(2,1)S(1)} %copy.94), channel_id=1, source_target_pairs={{8,0},{16,8},{24,16},{9,1},{17,9},{25,17},{10,2},{18,10},{26,18},{... | collective-permute-start | bytes 86024 | tf_op jit(solution)/shard_map/ppermute | solution.py:320
  4.9 81.5 %collective-permute-start.3 = (bf16[224,16,4]{0,1,2:T(8,128)(2,1)S(1)}, bf16[224,16,4]{0,1,2:T(8,128)(2,1)S(1)}, u32[]{:S(2)}, u32[]{:S(2)}) collective-permute-start(bf16[224,16,4]{0,1,2:T(8,128)(2,1)S(1)} %copy.95), channel_id=1, source_target_pairs={{0,8},{8,16},{16,24},{1,9},{9,17},{17,25},{2,10},{10,18},{18,26},{... | collective-permute-start | bytes 86024 | tf_op jit(solution)/shard_map/ppermute | solution.py:320
  14.5 81.2 %collective-permute-start = (bf16[224,4,512]{2,1,0:T(4,128)(2,1)}, bf16[224,4,512]{2,1,0:T(4,128)(2,1)}, u32[]{:S(2)}, u32[]{:S(2)}) collective-permute-start(bf16[224,4,512]{2,1,0:T(4,128)(2,1)} %get-tuple-element.25), channel_id=1, source_target_pairs={{0,1},{1,2},{2,3},{3,4},{4,5},{5,6},{6,7},{8,9},{9,10},{10,11},{11... | collective-permute-start | bytes 2752520 | tf_op jit(solution)/shard_map/ppermute | solution.py:320
  16.9 78.9 %collective-permute-start.1 = (bf16[224,4,512]{2,1,0:T(4,128)(2,1)}, bf16[224,4,512]{2,1,0:T(4,128)(2,1)}, u32[]{:S(2)}, u32[]{:S(2)}) collective-permute-start(bf16[224,4,512]{2,1,0:T(4,128)(2,1)} %get-tuple-element.26), channel_id=1, source_target_pairs={{1,0},{2,1},{3,2},{4,3},{5,4},{6,5},{7,6},{9,8},{10,9},{11,10},{12... | collective-permute-start | bytes 2752520 | tf_op jit(solution)/shard_map/ppermute | solution.py:320
  18.8 41.1 %copy-start.10 = (f32[80,80]{1,0:T(8,128)S(1)}, f32[80,80]{1,0:T(8,128)}, u32[]{:S(2)}) copy-start(f32[80,80]{1,0:T(8,128)} %constant.200) | copy-start | bytes 76804
  18.8 41.1 %copy-start.11 = (f32[80,80]{1,0:T(8,128)S(1)}, f32[80,80]{1,0:T(8,128)}, u32[]{:S(2)}) copy-start(f32[80,80]{1,0:T(8,128)} %constant.202) | copy-start | bytes 76804
  18.8 41.1 %copy-start.12 = (f32[80,80]{1,0:T(8,128)S(1)}, f32[80,80]{1,0:T(8,128)}, u32[]{:S(2)}) copy-start(f32[80,80]{1,0:T(8,128)} %constant.203) | copy-start | bytes 76804
  18.8 41.1 %copy-start.13 = (f32[80,80]{1,0:T(8,128)S(1)}, f32[80,80]{1,0:T(8,128)}, u32[]{:S(2)}) copy-start(f32[80,80]{1,0:T(8,128)} %constant.204) | copy-start | bytes 76804
  18.8 41.1 %copy-start.14 = (f32[80,80]{1,0:T(8,128)S(1)}, f32[80,80]{1,0:T(8,128)}, u32[]{:S(2)}) copy-start(f32[80,80]{1,0:T(8,128)} %constant.205) | copy-start | bytes 76804
  18.8 41.1 %copy-start.17 = (pred[80]{0:T(512)(128)(4,1)S(1)}, pred[80]{0:T(512)(128)(4,1)}, u32[]{:S(2)}) copy-start(pred[80]{0:T(512)(128)(4,1)} %constant.201) | copy-start | bytes 244
  86.5 7.8 %collective-permute-start.4 = (bf16[224,4,8]{0,2,1:T(8,128)(2,1)S(1)}, bf16[224,4,8]{0,2,1:T(8,128)(2,1)S(1)}, u32[]{:S(2)}, u32[]{:S(2)}) collective-permute-start(bf16[224,4,8]{0,2,1:T(8,128)(2,1)S(1)} %get-tuple-element.34), channel_id=1, source_target_pairs={{0,1},{1,2},{2,3},{3,4},{4,5},{5,6},{6,7},{8,9},{9,10},{10,11},{11... | collective-permute-start | bytes 43016 | tf_op jit(solution)/shard_map/ppermute | solution.py:320
  90.8 4.3 %collective-permute-start.5 = (bf16[224,4,8]{0,2,1:T(8,128)(2,1)S(1)}, bf16[224,4,8]{0,2,1:T(8,128)(2,1)S(1)}, u32[]{:S(2)}, u32[]{:S(2)}) collective-permute-start(bf16[224,4,8]{0,2,1:T(8,128)(2,1)S(1)} %get-tuple-element.33), channel_id=1, source_target_pairs={{1,0},{2,1},{3,2},{4,3},{5,4},{6,5},{7,6},{9,8},{10,9},{11,10},{12... | collective-permute-start | bytes 43016 | tf_op jit(solution)/shard_map/ppermute | solution.py:320
  95.8 2.9 %copy-start.2 = (bf16[224,16,512]{2,1,0:T(8,128)(2,1)S(1)}, bf16[224,16,512]{2,1,0:T(8,128)(2,1)}, u32[]{:S(2)}) copy-start(bf16[224,16,512]{2,1,0:T(8,128)(2,1)} %main_ref.1) | copy-start | bytes 11010052
  98.7 82.1 %copy-start.4 = (s32[16,512]{1,0:T(8,128)S(1)}, s32[16,512]{1,0:T(8,128)}, u32[]{:S(2)}) copy-start(s32[16,512]{1,0:T(8,128)} %mask_ref.3) | copy-start | bytes 98308
  182.4 1.8 copy-start
  184.1 0.7 copy-start.3
  274.8 2.0 copy-start.1

commit v2 on v1

--- a/solution.py
+++ b/solution.py
@@ -24,39 +24,39 @@
     return packed_in, packed_mid
 
 
-def tap_selector(out_order, in_order):
-    select = np.zeros((KSIZE, KSIZE * len(out_order), len(in_order)), np.float32)
-    for q in range(KSIZE):
-        for m, r in enumerate(out_order):
-            for k, s in enumerate(in_order):
-                if r is not None and s is not None and 0 <= s - r + REACH < KSIZE:
-                    select[s - r + REACH, q * len(out_order) + m, k] = 1.0
-    return select
-
-
-def tap_matrix(kernel, out_order, in_order, parts, width):
-    bands = kernel.shape[0]
+LOW_AT, NONE_AT, LANES = 32, 127, 128
+
+
+def tap_lanes(out_order, in_order, parts):
+    lanes = np.full((KSIZE * len(out_order), LANES), NONE_AT, np.int32)
+    for i, part in enumerate(parts):
+        base = LOW_AT if part == "low" else 0
+        for q in range(KSIZE):
+            for m, r in enumerate(out_order):
+                for k, s in enumerate(in_order):
+                    if r is not None and s is not None and 0 <= s - r + REACH < KSIZE:
+                        lanes[q * len(out_order) + m, i * len(in_order) + k] = (
+                            base + (s - r + REACH) * KSIZE + q
+                        )
+    return jnp.asarray(lanes)
+
+
+def tap_rows(kernel):
     high = lax.reduce_precision(kernel, 8, 7)
     low = kernel - high
-    one = tap_selector(out_order, in_order)
-    select = np.zeros((KSIZE, one.shape[1], width), np.float32)
-    is_low = np.zeros((1, 1, width), bool)
-    n = len(in_order)
-    for i, part in enumerate(parts):
-        select[:, :, i * n : (i + 1) * n] = one
-        is_low[:, :, i * n : (i + 1) * n] = part == "low"
-
-    def spread(taps, p):
-        row = taps[:, p * KSIZE : (p + 1) * KSIZE]
-        return jnp.repeat(row, len(out_order), axis=1)[:, :, None]
-
-    total = jnp.zeros((bands, one.shape[1], width), jnp.float32)
-    for p in range(KSIZE):
-        total = total + select[p][None] * jnp.where(is_low, spread(low, p), spread(high, p))
-    return total.astype(jnp.bfloat16)
-
-
-def smooth_kernel(main_ref, halo_ref, edge_ref, first_ref, second_ref, keep_ref, out_ref, hold):
+    count = kernel.shape[1]
+    row = jnp.pad(high, ((0, 0), (0, LOW_AT - count)))
+    return jnp.concatenate([row, jnp.pad(low, ((0, 0), (0, LANES - LOW_AT - count)))], axis=1)
+
+
+def tap_matrix(taps_ref, lanes_ref, b, width):
+    row = jnp.broadcast_to(taps_ref[pl.ds(b, 1), :], lanes_ref.shape)
+    matrix = jnp.take_along_axis(row, lanes_ref[...], axis=1, mode="promise_in_bounds")
+    return matrix.astype(jnp.bfloat16)[:, :width]
+
+
+def smooth_kernel(main_ref, halo_ref, edge_ref, one_ref, two_ref, first_ref, second_ref, keep_ref,
+                  out_ref, hold):
     rows, cols = main_ref.shape[1:]
     wide = cols + edge_ref.shape[2]
     mid = keep_ref.shape[0]
@@ -74,15 +74,17 @@
         main = jnp.concatenate([main_ref[b], edge_ref[b]], axis=1).astype(jnp.float32)
         packed = jnp.concatenate([main, halo_ref[b].astype(jnp.float32)], axis=0)
         packed = jnp.concatenate([packed, packed], axis=0).astype(jnp.bfloat16)
-        product = jnp.dot(first_ref[b], packed, preferred_element_type=jnp.float32)
+        product = jnp.dot(tap_matrix(one_ref, first_ref, b, packed.shape[0]), packed,
+                          preferred_element_type=jnp.float32)
         section = gather_columns(product, mid) * keep_ref[...]
         high = section.astype(jnp.bfloat16).astype(jnp.float32)
         low = section - high
-        spare = second_ref.shape[2] - 3 * mid
+        spare = -3 * mid % 16
         packed = jnp.concatenate(
             [high, low, high, jnp.zeros((spare, wide), jnp.float32)], axis=0
         ).astype(jnp.bfloat16)
-        product = jnp.dot(second_ref[b], packed, preferred_element_type=jnp.float32)
+        product = jnp.dot(tap_matrix(two_ref, second_ref, b, packed.shape[0]), packed,
+                          preferred_element_type=jnp.float32)
         result = gather_columns(product, rows)
         for j in range(cols // 128):
             hold[j, pl.ds(pl.multiple_of(b * rows, rows), rows), :] = result[:, j * 128 : j * 128 + 128]
@@ -96,7 +98,7 @@
             ].astype(jnp.bfloat16)
 
 
-def smooth_twice(radiance, halo, edge, first, second, keep):
+def smooth_twice(radiance, halo, edge, one, two, first, second, keep):
     bands, rows, cols = radiance.shape
 
     def band_block(array):
@@ -106,13 +108,14 @@
         smooth_kernel,
         grid=(bands // GROUP,),
         out_shape=jax.ShapeDtypeStruct((rows, bands, cols), jnp.bfloat16),
-        in_specs=[band_block(a) for a in (radiance, halo, edge, first, second)]
-        + [pl.BlockSpec(keep.shape, lambda i: (0, 0))],
+        in_specs=[band_block(a) for a in (radiance, halo, edge)]
+        + [pl.BlockSpec((GROUP, LANES), lambda i: (i, 0))] * 2
+        + [pl.BlockSpec(a.shape, lambda i: (0, 0)) for a in (first, second, keep)],
         out_specs=pl.BlockSpec((rows, GROUP, cols), lambda i: (0, i, 0)),
         scratch_shapes=[pltpu.VMEM((cols // 128, GROUP * rows, 128), jnp.float32)],
         compiler_params=pltpu.CompilerParams(vmem_limit_bytes=40 << 20),
         name="smooth_twice",
-    )(radiance, halo, edge, first, second, keep)
+    )(radiance, halo, edge, one, two, first, second, keep)
 
 
 def gram_kernel(x_ref, mask_ref, out_ref):
@@ -339,16 +342,17 @@
          widen(jnp.concatenate([corner_above, corner_below], axis=1))], axis=2)
 
     in_order, mid_order = row_orders(rows)
-    first = tap_matrix(kernel_one, mid_order, in_order, ("high", "low"), 2 * len(in_order))
-    packed = 3 * len(mid_order)
-    second = tap_matrix(kernel_two, list(range(rows)), mid_order, ("high", "high", "low"),
-                        packed + (-packed % 16))
+    first = tap_lanes(mid_order, in_order, ("high", "low"))
+    second = tap_lanes(list(range(rows)), mid_order, ("high", "high", "low"))
     row_at = jnp.asarray([0 if r is None else r for r in mid_order], jnp.int32)[:, None]
     col_at = jnp.arange(cols + 128, dtype=jnp.int32)[None, :]
     col_at = jnp.where(col_at < cols + 64, col_at, col_at - cols - 128)
     row_at, col_at = row_at + ml * rows, col_at + ma * cols
     keep = (row_at >= 0) & (row_at < nl * rows) & (col_at >= 0) & (col_at < na * cols)
-    smoothed = smooth_twice(radiance, halo, edge, first, second, keep.astype(jnp.float32))
+    smoothed = smooth_twice(
+        radiance, halo, edge, tap_rows(kernel_one), tap_rows(kernel_two), first, second,
+        keep.astype(jnp.float32),
+    )
 
     whole = sum_everywhere(local_gram(smoothed, usable_mask))
     gram, band_sum, count = whole[:bands, :bands], whole[bands, :bands], whole[bands, bands]

time: 280 us -> 220 us (0.79)
  other arithmetic: 128 us -> 62.6 us
  Pallas kernels: 112 us -> 119 us
    convert_element_type x2 -> x0, other arithmetic: 65.3 us -> none  [tap_matrix(): return total.astype(jnp.bfloat16)]
    pallas_call x1, Pallas kernels: 82.1 us -> 86 us  [smooth_twice(): pl.pallas_call(smooth_kernel, grid=(bands // GROUP,), out_shape=jax.Shape...]
    pallas_call x1, Pallas kernels: 25.3 us -> 28.1 us  [sum_everywhere(): pl.pallas_call(functools.partial(sum_kernel, na, nl), out_shape=jax.Shape...]
    unnamed x43 -> x25, local copies, waits for them, and re-layouts: 6.26 us -> 6.42 us
  transfers between devices with their start and end apart: 6 -> 6, of which waited for: 1 -> 1; matrix products, arithmetic and copies ran while one was open for 27% -> 4% of each run, Pallas kernels for 0% -> 0%
where the time goes in v2:
time: 220 us; the launch traced here: 219 us
  Pallas kernels  119 us (54%)
  other arithmetic  62.6 us (28%)
  local copies, waits for them, and re-layouts  16.5 us (8%)
  starting transfers between devices  16 us (7%)
  between operations  3.11 us (1%)
    pallas_call x1, Pallas kernels, smooth_twice(): pl.pallas_call(smooth_kernel, grid=(bands // GROUP,), out_shape=jax.Shape...  86 us
    another operation x7, other arithmetic, per_device(): lower = jnp.linalg.cholesky(loaded)  31.7 us
    pallas_call x1, Pallas kernels, sum_everywhere(): pl.pallas_call(functools.partial(sum_kernel, na, nl), out_shape=jax.Shape...  28.1 us
    another operation x6, other arithmetic, per_device(): lax.linalg.triangular_solve(lower, jnp.eye(bands, dtype=jnp.float32), lef...  20 us
    ppermute x3, starting transfers between devices, from_sides(): lax.ppermute(high_edge, axis, forward)  12.1 us
    unnamed x25, local copies, waits for them, and re-layouts  6.42 us
  transfers between devices with their start and end apart: 6, of which 1 were waited for; matrix products, arithmetic and copies ran while one was open for 4% of the time, Pallas kernels for 0%

profile of v2, /device:TPU:0, one launch (start us, length us, event | category | flops | bytes accessed | tf_op | source)
XLA Modules:
  0.0 219.2 jit_solution(5831110325371390458)
XLA Ops:
  0.0 1.9 fusion.16
  1.9 0.8 copy.53
  2.8 1.3 collective-permute-start.2
  4.0 0.8 copy.54
  4.9 5.5 %collective-permute-start.3 = (bf16[224,16,4]{0,1,2:T(8,128)(2,1)S(1)}, bf16[224,16,4]{0,1,2:T(8,128)(2,1)S(1)}, u32[]{:S(2)}, u32[]{:S(2)}) collective-permute-start(bf16[224,16,4]{0,1,2:T(8,128)(2,1)S(1)} %copy.54), channel_id=1, source_target_pairs={{0,8},{8,16},{16,24},{1,9},{9,17},{17,25},{2,10},{10,18},{18,26},{... | collective-permute-start | bytes 86024 | tf_op jit(solution)/shard_map/ppermute | solution.py:323
  10.3 4.0 %fusion.15 = (bf16[224,4,512]{2,1,0:T(4,128)(2,1)}, bf16[224,4,512]{2,1,0:T(4,128)(2,1)}) fusion(bf16[224,16,512]{2,1,0:T(8,128)(2,1)} %main_ref.1), kind=kLoop, calls=%fused_computation.60 | loop fusion | bytes 3670016 | tf_op jit(solution)/shard_map/slice | solution.py:331
  14.3 2.4 %collective-permute-start = (bf16[224,4,512]{2,1,0:T(4,128)(2,1)}, bf16[224,4,512]{2,1,0:T(4,128)(2,1)}, u32[]{:S(2)}, u32[]{:S(2)}) collective-permute-start(bf16[224,4,512]{2,1,0:T(4,128)(2,1)} %get-tuple-element.25), channel_id=1, source_target_pairs={{0,1},{1,2},{2,3},{3,4},{4,5},{5,6},{6,7},{8,9},{9,10},{10,11},{11... | collective-permute-start | bytes 2752520 | tf_op jit(solution)/shard_map/ppermute | solution.py:323
  16.7 1.3 collective-permute-start.1
  18.0 0.1 copy.45
  18.2 0.1 copy.48
  18.3 0.1 copy.44
  18.4 0.1 copy.47
  18.6 0.1 select_maximum_fusion
  19.1 4.3 %collective-permute-start.4 = (bf16[224,4,8]{0,2,1:T(8,128)(2,1)S(1)}, bf16[224,4,8]{0,2,1:T(8,128)(2,1)S(1)}, u32[]{:S(2)}, u32[]{:S(2)}) collective-permute-start(bf16[224,4,8]{0,2,1:T(8,128)(2,1)S(1)} %get-tuple-element.34), channel_id=1, source_target_pairs={{0,1},{1,2},{2,3},{3,4},{4,5},{5,6},{6,7},{8,9},{9,10},{10,11},{11... | collective-permute-start | bytes 43016 | tf_op jit(solution)/shard_map/ppermute | solution.py:323
  23.4 1.3 collective-permute-start.5
  24.7 0.8 copy.42
  25.5 0.8 copy.43
  26.3 0.6 pad_maximum_fusion.1.edge_ref
  26.9 0.8 collective-permute-done.5
  27.7 0.3 copy.40
  28.1 0.3 copy.41
  28.4 2.9 %pad_maximum_fusion.halo_ref = bf16[224,8,640]{2,1,0:T(8,128)(2,1)S(1)} fusion(bf16[224,8,4]{2,1,0:T(8,128)(2,1)S(1)} %copy.41, bf16[224,8,4]{2,1,0:T(8,128)(2,1)S(1)} %copy.40, bf16[224,4,512]{2,1,0:T(4,128)(2,1)} %collective-permute-done.1, bf16[224,4,512]{2,1,0:T(4,128)(2,1)} %collective-permute-done, bf16[640]{0:T(1024)(128)(2,1)S(1)} %pad.42.clone), kind=kLoop, calls=%fused_computation | loop fusion | flops 11468800 | bytes 4158720 | tf_op jit(solution)/shard_map/concatenate | solution.py:340
  31.4 86.0 %smooth_twice.1.x_ref = bf16[16,224,512]{2,1,0:T(8,128)(2,1)S(1)} custom-call(bf16[224,16,512]{2,1,0:T(8,128)(2,1)S(1)} %copy-done.2, bf16[224,8,640]{2,1,0:T(8,128)(2,1)S(1)} %pad_maximum_fusion.halo_ref, bf16[224,16,128]{2,1,0:T(8,128)(2,1)S(1)} %pad_maximum_fusion.1.edge_ref, f32[224,128]{1,0:T(8,128)S(1)} %get-tuple-element.44.one_ref, ...), custom_call_target="tpu_custom_call" | custom-call | tf_op jit(solution)/shard_map/smooth_twice/pallas_call | solution.py:107
  117.4 1.5 local_gram.1.x_ref
  118.9 1.8 copy-done
  120.7 0.7 copy-done.3
  121.4 28.1 %sum_everywhere.1 = f32[256,256]{1,0:T(8,128)} custom-call(f32[256,256]{1,0:T(8,128)} %copy-done.3), custom_call_target="tpu_custom_call" | custom-call | tf_op jit(solution)/shard_map/sum_everywhere/pallas_call | solution.py:265
  149.5 1.3 slice.87
  150.8 1.3 slice_divide_fusion
  152.8 2.3 %select_reduce_fusion = f32[]{:T(128)} fusion(f32[]{:T(128)S(6)} %sub.28, f32[224]{0:T(256)S(1)} %bitcast.34, f32[]{:T(128)} %bitcast, f32[256,256]{1,0:T(8,128)} %sum_everywhere.1), kind=kLoop, calls=%fused_computation.13 | loop fusion | flops 351231 | bytes 202764 | tf_op jit(solution)/shard_map/jit(trace)/reduce_sum | solution.py:361
  155.8 1.7 select_add_fusion
  157.5 0.1 copy.50
  157.6 1.7 fusion.1
  159.3 11.7 %cholesky.50 = f32[128,128]{1,0:T(8,128)S(1)} custom-call(f32[128,128]{1,0:T(8,128)S(1)} %cholesky.121), custom_call_target="Cholesky" | custom-call | tf_op jit(solution)/shard_map/jit(cholesky)/cholesky | solution.py:363
  171.1 9.8 %custom-call.14 = f32[1,128,128]{1,2,0:T(8,128)S(1)} custom-call(f32[1,128,128]{2,1,0:T(8,128)S(1)} %get-tuple-element.32), custom_call_target="InvertDiagBlocksLowerTriangular" | custom-call | tf_op jit(solution)/shard_map/jit(cholesky)/cholesky | solution.py:363
  180.9 0.2 constant_dynamic-update-slice_fusion.3
  181.1 0.2 convolution_subtract_fusion.1
  181.4 8.8 %cholesky.108 = f32[96,96]{1,0:T(8,128)S(1)} custom-call(f32[96,96]{1,0:T(8,128)S(1)} %convolution_subtract_fusion.1), custom_call_target="Cholesky" | custom-call | tf_op jit(solution)/shard_map/jit(cholesky)/cholesky | solution.py:363
  190.2 0.7 compare_reduce_fusion
  190.8 0.6 compare_reduce_fusion.1
  192.9 19.9 %custom-call.15 = f32[2,128,128]{1,2,0:T(8,128)S(1)} custom-call(f32[2,128,128]{2,1,0:T(8,128)S(1)} %pad_maximum_fusion.4), custom_call_target="InvertDiagBlocksLowerTriangular" | custom-call | tf_op jit(solution)/shard_map/triangular_solve | solution.py:364
  212.8 0.3 fusion.2
  213.1 0.4 convolution_subtract_fusion
  213.5 0.1 copy.51
  213.6 0.3 fusion.8
  213.9 0.3 convolution_bitcast_fusion.shift_ref
  214.3 2.0 copy-done.1
  216.3 2.9 %score.1 = f32[16,512]{1,0:T(8,128)} custom-call(bf16[224,224]{1,0:T(8,128)(2,1)S(1)} %get-tuple-element.30.high_ref, bf16[224,224]{1,0:T(8,128)(2,1)S(1)} %get-tuple-element.29.low_ref, f32[224,1]{1,0:T(8,128)S(1)} %convolution_bitcast_fusion.shift_ref, bf16[16,224,512]{2,1,0:T(8,128)(2,1)S(1)} %copy-done.1, s32[16,512]{1,0:T(8,128)S(1)} %copy-done.4), custom_call_target="tpu_custom_call" | custom-call | tf_op jit(solution)/shard_map/score/pallas_call | solution.py:305
  (51 shorter events, 0.7 us)
Async XLA Ops:
  1.9 16.1 %copy-start.7 = (f32[224,25]{0,1:T(8,128)S(1)}, f32[224,25]{0,1:T(8,128)}, u32[]{:S(2)}) copy-start(f32[224,25]{0,1:T(8,128)} %param.8) | copy-start | bytes 67204
  1.9 16.2 %copy-start.8 = (f32[224,25]{0,1:T(8,128)S(1)}, f32[224,25]{0,1:T(8,128)}, u32[]{:S(2)}) copy-start(f32[224,25]{0,1:T(8,128)} %param.9) | copy-start | bytes 67204
  1.9 16.8 %copy-start.9 = (s32[24]{0:T(128)S(1)}, s32[24]{0:T(128)}, u32[]{:S(2)}) copy-start(s32[24]{0:T(128)} %constant.134.clone) | copy-start | bytes 292
  2.8 16.3 %collective-permute-start.2 = (bf16[224,16,4]{0,1,2:T(8,128)(2,1)S(1)}, bf16[224,16,4]{0,1,2:T(8,128)(2,1)S(1)}, u32[]{:S(2)}, u32[]{:S(2)}) collective-permute-start(bf16[224,16,4]{0,1,2:T(8,128)(2,1)S(1)} %copy.53), channel_id=1, source_target_pairs={{8,0},{16,8},{24,16},{9,1},{17,9},{25,17},{10,2},{18,10},{26,18},{... | collective-permute-start | bytes 86024 | tf_op jit(solution)/shard_map/ppermute | solution.py:323
  4.9 14.2 %collective-permute-start.3 = (bf16[224,16,4]{0,1,2:T(8,128)(2,1)S(1)}, bf16[224,16,4]{0,1,2:T(8,128)(2,1)S(1)}, u32[]{:S(2)}, u32[]{:S(2)}) collective-permute-start(bf16[224,16,4]{0,1,2:T(8,128)(2,1)S(1)} %copy.54), channel_id=1, source_target_pairs={{0,8},{8,16},{16,24},{1,9},{9,17},{17,25},{2,10},{10,18},{18,26},{... | collective-permute-start | bytes 86024 | tf_op jit(solution)/shard_map/ppermute | solution.py:323
  14.3 14.1 %collective-permute-start = (bf16[224,4,512]{2,1,0:T(4,128)(2,1)}, bf16[224,4,512]{2,1,0:T(4,128)(2,1)}, u32[]{:S(2)}, u32[]{:S(2)}) collective-permute-start(bf16[224,4,512]{2,1,0:T(4,128)(2,1)} %get-tuple-element.25), channel_id=1, source_target_pairs={{0,1},{1,2},{2,3},{3,4},{4,5},{5,6},{6,7},{8,9},{9,10},{10,11},{11... | collective-permute-start | bytes 2752520 | tf_op jit(solution)/shard_map/ppermute | solution.py:323
  16.7 11.7 %collective-permute-start.1 = (bf16[224,4,512]{2,1,0:T(4,128)(2,1)}, bf16[224,4,512]{2,1,0:T(4,128)(2,1)}, u32[]{:S(2)}, u32[]{:S(2)}) collective-permute-start(bf16[224,4,512]{2,1,0:T(4,128)(2,1)} %get-tuple-element.26), channel_id=1, source_target_pairs={{1,0},{2,1},{3,2},{4,3},{5,4},{6,5},{7,6},{9,8},{10,9},{11,10},{12... | collective-permute-start | bytes 2752520 | tf_op jit(solution)/shard_map/ppermute | solution.py:323
  19.1 7.8 %collective-permute-start.4 = (bf16[224,4,8]{0,2,1:T(8,128)(2,1)S(1)}, bf16[224,4,8]{0,2,1:T(8,128)(2,1)S(1)}, u32[]{:S(2)}, u32[]{:S(2)}) collective-permute-start(bf16[224,4,8]{0,2,1:T(8,128)(2,1)S(1)} %get-tuple-element.34), channel_id=1, source_target_pairs={{0,1},{1,2},{2,3},{3,4},{4,5},{5,6},{6,7},{8,9},{9,10},{10,11},{11... | collective-permute-start | bytes 43016 | tf_op jit(solution)/shard_map/ppermute | solution.py:323
  23.4 4.3 %collective-permute-start.5 = (bf16[224,4,8]{0,2,1:T(8,128)(2,1)S(1)}, bf16[224,4,8]{0,2,1:T(8,128)(2,1)S(1)}, u32[]{:S(2)}, u32[]{:S(2)}) collective-permute-start(bf16[224,4,8]{0,2,1:T(8,128)(2,1)S(1)} %get-tuple-element.33), channel_id=1, source_target_pairs={{1,0},{2,1},{3,2},{4,3},{5,4},{6,5},{7,6},{9,8},{10,9},{11,10},{12... | collective-permute-start | bytes 43016 | tf_op jit(solution)/shard_map/ppermute | solution.py:323
  26.9 4.5 %copy-start.5 = (s32[120,128]{1,0:T(8,128)S(1)}, s32[120,128]{1,0:T(8,128)}, u32[]{:S(2)}) copy-start(s32[120,128]{1,0:T(8,128)} %constant.132.clone.first_ref) | copy-start | bytes 184324
  26.9 4.5 %copy-start.6 = (s32[80,128]{1,0:T(8,128)S(1)}, s32[80,128]{1,0:T(8,128)}, u32[]{:S(2)}) copy-start(s32[80,128]{1,0:T(8,128)} %constant.133.clone.second_ref) | copy-start | bytes 122884
  28.4 3.0 %copy-start.2 = (bf16[224,16,512]{2,1,0:T(8,128)(2,1)S(1)}, bf16[224,16,512]{2,1,0:T(8,128)(2,1)}, u32[]{:S(2)}) copy-start(bf16[224,16,512]{2,1,0:T(8,128)(2,1)} %main_ref.1) | copy-start | bytes 11010052
  31.3 86.0 %copy-start.4 = (s32[16,512]{1,0:T(8,128)S(1)}, s32[16,512]{1,0:T(8,128)}, u32[]{:S(2)}) copy-start(s32[16,512]{1,0:T(8,128)} %mask_ref.3) | copy-start | bytes 98308
  118.9 1.8 copy-start
  120.7 0.7 copy-start.3
  214.2 2.0 copy-start.1
